TPU v7x, 32 devices: a whole 2x2x4 slice. The times are simulated.
32 devices in a mesh: table: 4 (over x, core), row: 8 (over z, y).
Axes of the slice: x: 2, y: 2, z: 4, core: 2. Of those that a mesh axis runs over, the one named last changes fastest.
Arguments:
- features: bfloat16 [4096, 4096], P('row', 'table'), may hold values from -6 to 6
- cotangent: bfloat16 [4096, 4096], P('row', 'table'), may hold values from -6 to 6
- cross_in: bfloat16 [4096, 512], P('table'), may hold values from -0.09375 to 0.09375
- cross_out: bfloat16 [4096, 512], P('table'), may hold values from -0.25 to 0.25
- bias: float32 [4096], P('table'), may hold values from -6 to 6
- dest_shard: int32 [32, 4096, 1], P('table', 'row'), may hold values from 0 to 7; in each aligned block of 512 rows (0 to 511, 512 to 1023, ..., all dimensions but the last counted through in order) at most 96 rows name the same one
- quot_row: int32 [32, 4096], P('table', 'row'), may hold values from 0 to 1023
- rem_row: int32 [32, 4096], P('table', 'row'), may hold values from 0 to 2047
- quot_slab: bfloat16 [32, 8192, 128], P('table', 'row'), may hold values from -6 to 6
- quot_accum: float32 [32, 8192], P('table', 'row'), may hold values from 0.05 to 2
- rem_table: bfloat16 [32, 2048, 128], P('table'), may hold values from -6 to 6
- rem_accum: float32 [32, 2048], P('table'), may hold values from 0.5 to 20
Outputs:
- quot_out: bfloat16 [32, 8192, 128], P('table', 'row')
- quot_acc_out: float32 [32, 8192], P('table', 'row')
- rem_out: bfloat16 [32, 2048, 128], P('table')
- rem_acc_out: float32 [32, 2048], P('table', 'row')
Inputs may be any that keep to these rules, and one draw needn't show every extreme that they name: `dest_shard`: for each table, the 512 samples of one index of row name one row shard at most 96 times, a bound that some block reaches.
All inputs are finite; a program needn't handle non-finite values.
Results may differ from a plain program's by a relative error of at most 0.004.
Values may be sent and summed in bfloat16 or wider, within the bound.
A program may use at most 128 MiB of HBM per device.

v0:
```python
import jax
import jax.numpy as jnp
from jax import lax
from jax.sharding import PartitionSpec as P

step_rate = 0.3
epsilon = 1e-06


def table_grads(items):
    grads, keys, slab, rtab = items
    rem_count = rtab.shape[0]
    qlocal = keys // rem_count
    rlocal = keys % rem_count
    q_hot = (qlocal[:, None] == jnp.arange(slab.shape[0], dtype=jnp.int32)[None, :]).astype(
        jnp.bfloat16
    )
    r_hot = (rlocal[:, None] == jnp.arange(rem_count, dtype=jnp.int32)[None, :]).astype(
        jnp.bfloat16
    )
    rem_pick = jnp.dot(r_hot, rtab, preferred_element_type=jnp.float32)
    quot_pick = jnp.dot(q_hot, slab, preferred_element_type=jnp.float32)
    grad_f = grads.astype(jnp.float32)
    over_rows = (((0,), (0,)), ((), ()))
    grad_q = lax.dot_general(
        q_hot.astype(jnp.float32),
        grad_f * rem_pick,
        over_rows,
        precision=lax.Precision.HIGHEST,
        preferred_element_type=jnp.float32,
    )
    grad_r = lax.dot_general(
        r_hot.astype(jnp.float32),
        grad_f * quot_pick,
        over_rows,
        precision=lax.Precision.HIGHEST,
        preferred_element_type=jnp.float32,
    )
    return (grad_q, grad_r)


def per_device(
    features,
    cotangent,
    cross_in,
    cross_out,
    bias,
    dest_shard,
    quot_row,
    rem_row,
    quot_slab,
    quot_accum,
    rem_table,
    rem_accum,
):
    contract = (((1,), (1,)), ((), ()))
    samples = features.shape[0]
    tables_dev = quot_slab.shape[0]
    row_width = quot_slab.shape[2]
    rem_rows = rem_table.shape[1]
    row_count = lax.axis_size("row")
    capacity = 3 * samples // (2 * row_count)
    slots = row_count * capacity
    product = (cotangent.astype(jnp.float32) * features.astype(jnp.float32)).astype(jnp.bfloat16)
    rank_left = jnp.dot(features, cross_in, preferred_element_type=jnp.float32)
    rank_right = jnp.dot(product, cross_out, preferred_element_type=jnp.float32)
    rank_left, rank_right = lax.psum((rank_left, rank_right), "table")
    cross_gate = (
        lax.dot_general(
            rank_left.astype(jnp.bfloat16), cross_out, contract, preferred_element_type=jnp.float32
        )
        + bias
    )
    cross_back = lax.dot_general(
        rank_right.astype(jnp.bfloat16), cross_in, contract, preferred_element_type=jnp.float32
    )
    pooled = (cotangent.astype(jnp.float32) * (cross_gate + 1.0) + cross_back).astype(jnp.bfloat16)
    pooled = pooled.reshape(samples, tables_dev, row_width)
    target = dest_shard[:, :, 0]
    onehot = target[:, :, None] == jnp.arange(row_count, dtype=jnp.int32)[None, None, :]
    lower = (
        jnp.arange(samples, dtype=jnp.int32)[:, None]
        >= jnp.arange(samples, dtype=jnp.int32)[None, :]
    ).astype(jnp.bfloat16)
    running = jnp.einsum(
        "ij,tjn->tin", lower, onehot.astype(jnp.bfloat16), preferred_element_type=jnp.float32
    )
    slot_index = jnp.sum(jnp.where(onehot, running, 0.0), axis=2).astype(jnp.int32) - 1
    position = target * capacity + slot_index
    placed = position[:, :, None] == jnp.arange(slots, dtype=jnp.int32)[None, None, :]
    send_rows = jnp.einsum(
        "tsk,ste->tke", placed.astype(jnp.bfloat16), pooled, preferred_element_type=jnp.float32
    ).astype(jnp.bfloat16)
    key_words = quot_row * rem_rows + rem_row
    send_keys = jnp.sum(jnp.where(placed, key_words[:, :, None], 0), axis=1)
    send_rows = send_rows.reshape(tables_dev, row_count, capacity, row_width)
    send_keys = send_keys.reshape(tables_dev, row_count, capacity)
    got_rows, got_keys = (
        lax.all_to_all(send_rows, "row", split_axis=1, concat_axis=1, tiled=True),
        lax.all_to_all(send_keys, "row", split_axis=1, concat_axis=1, tiled=True),
    )
    got_rows = got_rows.reshape(tables_dev, slots, row_width)
    got_keys = got_keys.reshape(tables_dev, slots)
    quot_grad, rem_grad = lax.map(table_grads, (got_rows, got_keys, quot_slab, rem_table))
    quot_acc_out = quot_accum + jnp.mean(quot_grad * quot_grad, axis=-1)
    quot_out = (
        quot_slab.astype(jnp.float32)
        - step_rate * quot_grad * lax.rsqrt(quot_acc_out + epsilon)[..., None]
    ).astype(jnp.bfloat16)
    share = rem_rows // row_count
    start = lax.axis_index("row") * share
    rem_part = lax.psum_scatter(rem_grad, "row", scatter_dimension=1, tiled=True)
    old_rows = lax.dynamic_slice_in_dim(rem_table, start, share, 1)
    old_accum = lax.dynamic_slice_in_dim(rem_accum, start, share, 1)
    rem_acc_out = old_accum + jnp.mean(rem_part * rem_part, axis=-1)
    fresh_rows = (
        old_rows.astype(jnp.float32)
        - step_rate * rem_part * lax.rsqrt(rem_acc_out + epsilon)[..., None]
    ).astype(jnp.bfloat16)
    rem_out = lax.all_gather(fresh_rows, "row", axis=1, tiled=True)
    return (quot_out, quot_acc_out, rem_out, rem_acc_out)


def solution(mesh):
    placed = (
        P("row", "table"),
        P("row", "table"),
        P("table", None),
        P("table", None),
        P("table"),
        P("table", "row", None),
        P("table", "row"),
        P("table", "row"),
        P("table", "row", None),
        P("table", "row"),
        P("table", None, None),
        P("table", None),
    )
    return jax.shard_map(
        per_device,
        mesh=mesh,
        in_specs=placed,
        out_specs=(
            P("table", "row", None),
            P("table", "row"),
            P("table", None, None),
            P("table", "row"),
        ),
        check_vma=False,
    )
```

profile of v0, /device:TPU:0, one launch (start us, length us, event | category | flops | bytes accessed | tf_op | source)
XLA Modules:
  0.0 462.2 jit_solution(11304062984709523501)
XLA Ops:
  9.8 1.6 select_reduce_fusion
  12.1 7.3 %all-to-all-start = ((s32[8,8,96]{2,0,1:T(8,128)}), s32[8,8,96]{2,0,1:T(8,128)S(1)}, u32[]{:S(2)}, u32[]{:S(2)}) async-start(s32[8,8,96]{2,0,1:T(8,128)} %copy.19), calls=%async_computation | async-start | bytes 65536 | tf_op jit(solution)/shard_map/all_to_all | solution.py:100
  19.4 2.4 fusion.41
  22.6 41.2 %all-reduce.2 = (bf16[512,512]{1,0:T(8,128)(2,1)}, bf16[512,512]{1,0:T(8,128)(2,1)}) all-reduce(f32[512,512]{1,0:T(8,128)S(1)} %fusion.41, f32[512,512]{1,0:T(8,128)S(1)} %fusion.31), channel_id=1, replica_groups=mesh['table'=4,'row'=8] {'table'}, use_global_device_ids=true, to_apply=%region_1.0 | all-reduce | flops 524288 | bytes 3145728 | tf_op jit(solution)/shard_map/psum | solution.py:67
  63.7 1.9 fusion.42
  66.5 2.2 fusion.27
  70.0 5.3 %all-to-all-start.1 = ((bf16[8,8,96,128]{3,2,0,1:T(8,128)(2,1)}), bf16[8,8,96,128]{3,2,0,1:T(8,128)(2,1)S(1)}, u32[]{:S(2)}, u32[]{:S(2)}) async-start(bf16[8,8,96,128]{3,2,0,1:T(8,128)(2,1)} %copy.22), calls=%async_computation.1 | async-start | bytes 3145728 | tf_op jit(solution)/shard_map/all_to_all | solution.py:99
  75.6 37.7 %all-to-all-done.1 = bf16[8,8,96,128]{3,2,0,1:T(8,128)(2,1)S(1)} async-done(((bf16[8,8,96,128]{3,2,0,1:T(8,128)(2,1)}), bf16[8,8,96,128]{3,2,0,1:T(8,128)(2,1)S(1)}, u32[]{:S(2)}, u32[]{:S(2)}) %all-to-all-start.1) | async-done | bytes 1572896 | tf_op jit(solution)/shard_map/all_to_all | solution.py:99
  114.6 110.0 %while.14 = (s32[]{:T(128)}, f32[8,1024,128]{2,1,0:T(8,128)}, f32[8,2048,128]{2,1,0:T(8,128)}, s32[8,768]{1,0:T(8,128)S(1)}, bf16[8,768,128]{2,1,0:T(8,128)(2,1)...) while((s32[]{:T(128)}, f32[8,1024,128]{2,1,0:T(8,128)}, ...), condition=%wide.region_5.6_spmd, body=%wide.region_4.5_spmd.sunk | while | flops 4232984832 | bytes 4355177 | solution.py:104
  114.6 2.3 fusion.64
  116.9 3.6 fusion.65
  120.4 1.7 fusion.66
  122.1 6.2 %fusion.67 = f32[8,2048,128]{2,1,0:T(8,128)} fusion(f32[8,2048,128]{2,1,0:T(8,128)} %get-tuple-element.178, s32[]{:T(128)S(6)} %copy.42, f32[768,128]{1,0:T(8,128)S(1)} %fusion.66, s32[768]{0:T(1024)S(1)} %get-tuple-element.166), kind=kOutput, calls=%fused_computation.9.clone.1 | convolution fusion | flops 2417491968 | bytes 1444868 | tf_op jit(solution)/shard_map/while/body/eval_jaxpr/dot_general | solution.py:32
  128.3 2.3 fusion.64
  130.6 3.6 fusion.65
  134.2 1.7 fusion.66
  135.9 6.2 %fusion.67 = f32[8,2048,128]{2,1,0:T(8,128)} fusion(f32[8,2048,128]{2,1,0:T(8,128)} %get-tuple-element.178, s32[]{:T(128)S(6)} %copy.42, f32[768,128]{1,0:T(8,128)S(1)} %fusion.66, s32[768]{0:T(1024)S(1)} %get-tuple-element.166), kind=kOutput, calls=%fused_computation.9.clone.1 | convolution fusion | flops 2417491968 | bytes 1444868 | tf_op jit(solution)/shard_map/while/body/eval_jaxpr/dot_general | solution.py:32
  142.1 2.3 fusion.64
  144.4 3.6 fusion.65
  147.9 1.7 fusion.66
  149.6 6.2 %fusion.67 = f32[8,2048,128]{2,1,0:T(8,128)} fusion(f32[8,2048,128]{2,1,0:T(8,128)} %get-tuple-element.178, s32[]{:T(128)S(6)} %copy.42, f32[768,128]{1,0:T(8,128)S(1)} %fusion.66, s32[768]{0:T(1024)S(1)} %get-tuple-element.166), kind=kOutput, calls=%fused_computation.9.clone.1 | convolution fusion | flops 2417491968 | bytes 1444868 | tf_op jit(solution)/shard_map/while/body/eval_jaxpr/dot_general | solution.py:32
  155.9 2.3 fusion.64
  158.1 3.6 fusion.65
  161.7 1.7 fusion.66
  163.4 6.2 %fusion.67 = f32[8,2048,128]{2,1,0:T(8,128)} fusion(f32[8,2048,128]{2,1,0:T(8,128)} %get-tuple-element.178, s32[]{:T(128)S(6)} %copy.42, f32[768,128]{1,0:T(8,128)S(1)} %fusion.66, s32[768]{0:T(1024)S(1)} %get-tuple-element.166), kind=kOutput, calls=%fused_computation.9.clone.1 | convolution fusion | flops 2417491968 | bytes 1444868 | tf_op jit(solution)/shard_map/while/body/eval_jaxpr/dot_general | solution.py:32
  169.6 2.3 fusion.64
  171.9 3.6 fusion.65
  175.4 1.7 fusion.66
  177.1 6.2 %fusion.67 = f32[8,2048,128]{2,1,0:T(8,128)} fusion(f32[8,2048,128]{2,1,0:T(8,128)} %get-tuple-element.178, s32[]{:T(128)S(6)} %copy.42, f32[768,128]{1,0:T(8,128)S(1)} %fusion.66, s32[768]{0:T(1024)S(1)} %get-tuple-element.166), kind=kOutput, calls=%fused_computation.9.clone.1 | convolution fusion | flops 2417491968 | bytes 1444868 | tf_op jit(solution)/shard_map/while/body/eval_jaxpr/dot_general | solution.py:32
  183.3 2.3 fusion.64
  185.6 3.6 fusion.65
  189.2 1.7 fusion.66
  190.9 6.2 %fusion.67 = f32[8,2048,128]{2,1,0:T(8,128)} fusion(f32[8,2048,128]{2,1,0:T(8,128)} %get-tuple-element.178, s32[]{:T(128)S(6)} %copy.42, f32[768,128]{1,0:T(8,128)S(1)} %fusion.66, s32[768]{0:T(1024)S(1)} %get-tuple-element.166), kind=kOutput, calls=%fused_computation.9.clone.1 | convolution fusion | flops 2417491968 | bytes 1444868 | tf_op jit(solution)/shard_map/while/body/eval_jaxpr/dot_general | solution.py:32
  197.1 2.3 fusion.64
  199.4 3.6 fusion.65
  202.9 1.7 fusion.66
  204.6 6.2 %fusion.67 = f32[8,2048,128]{2,1,0:T(8,128)} fusion(f32[8,2048,128]{2,1,0:T(8,128)} %get-tuple-element.178, s32[]{:T(128)S(6)} %copy.42, f32[768,128]{1,0:T(8,128)S(1)} %fusion.66, s32[768]{0:T(1024)S(1)} %get-tuple-element.166), kind=kOutput, calls=%fused_computation.9.clone.1 | convolution fusion | flops 2417491968 | bytes 1444868 | tf_op jit(solution)/shard_map/while/body/eval_jaxpr/dot_general | solution.py:32
  210.9 2.3 fusion.64
  213.1 3.6 fusion.65
  216.7 1.7 fusion.66
  218.4 6.2 %fusion.67 = f32[8,2048,128]{2,1,0:T(8,128)} fusion(f32[8,2048,128]{2,1,0:T(8,128)} %get-tuple-element.178, s32[]{:T(128)S(6)} %copy.42, f32[768,128]{1,0:T(8,128)S(1)} %fusion.66, s32[768]{0:T(1024)S(1)} %get-tuple-element.166), kind=kOutput, calls=%fused_computation.9.clone.1 | convolution fusion | flops 2417491968 | bytes 1444868 | tf_op jit(solution)/shard_map/while/body/eval_jaxpr/dot_general | solution.py:32
  224.9 147.9 %reduce-scatter.2.cloned.1.call-done = f32[8,256,128]{2,1,0:T(8,128)} async-done(((f32[8,2048,128]{2,1,0:T(8,128)}), f32[8,256,128]{2,1,0:T(8,128)}) %reduce-scatter.2.cloned.1.call-update) | async-done | bytes 1048592 | tf_op jit(solution)/shard_map/reduce_scatter | solution.py:112
  372.8 1.6 multiply_reduce_fusion.1
  375.7 2.7 subtract_convert_fusion.1
  378.4 3.5 multiply_reduce_fusion
  382.5 2.2 subtract_convert_fusion
  384.7 66.2 %all-gather.2.cloned.1.call-done = bf16[8,2048,128]{2,1,0:T(8,128)(2,1)} async-done(((bf16[8,256,128]{2,1,0:T(8,128)(2,1)}), bf16[8,2048,128]{2,1,0:T(8,128)(2,1)}) %all-gather.2.cloned.1.call-update) | async-done | bytes 4194320 | tf_op jit(solution)/shard_map/all_gather | solution.py:120
  450.9 4.5 copy.51
  (59 shorter events, 10.2 us)
Async XLA Ops:
  7.2 14.6 %copy-start = (bf16[1024,512]{1,0:T(8,128)(2,1)S(1)}, bf16[1024,512]{1,0:T(8,128)(2,1)}, u32[]{:S(2)}) copy-start(bf16[1024,512]{1,0:T(8,128)(2,1)} %param.17) | copy-start | bytes 3145732
  12.1 57.9 %all-to-all-start = ((s32[8,8,96]{2,0,1:T(8,128)}), s32[8,8,96]{2,0,1:T(8,128)S(1)}, u32[]{:S(2)}, u32[]{:S(2)}) async-start(s32[8,8,96]{2,0,1:T(8,128)} %copy.19), calls=%async_computation | async-start | bytes 65536 | tf_op jit(solution)/shard_map/all_to_all | solution.py:100
  19.4 2.4 copy-start.3
  19.4 2.4 copy-start.4
  22.6 43.1 %copy-start.9 = (f32[1024]{0:T(1024)S(1)}, f32[1024]{0:T(1024)}, u32[]{:S(2)}) copy-start(f32[1024]{0:T(1024)} %param.18) | copy-start | bytes 12292
  63.7 2.0 copy-start.5
  63.7 2.0 copy-start.7
  63.7 2.0 copy-start.8
  70.0 43.3 %all-to-all-start.1 = ((bf16[8,8,96,128]{3,2,0,1:T(8,128)(2,1)}), bf16[8,8,96,128]{3,2,0,1:T(8,128)(2,1)S(1)}, u32[]{:S(2)}, u32[]{:S(2)}) async-start(bf16[8,8,96,128]{3,2,0,1:T(8,128)(2,1)} %copy.22), calls=%async_computation.1 | async-start | bytes 3145728 | tf_op jit(solution)/shard_map/all_to_all | solution.py:99
  75.3 297.5 %reduce-scatter.2.cloned.1.call-start = ((), (), s32[]{:S(2)}) async-start(), calls=%async_computation.3 | async-start | bytes 9437184 | tf_op jit(solution)/shard_map/reduce_scatter | solution.py:112
  224.6 226.3 %all-gather.2.cloned.1.call-start = ((), (), s32[]{:S(2)}) async-start(), calls=%async_computation.4 | async-start | bytes 4718592 | tf_op jit(solution)/shard_map/all_gather | solution.py:120
  375.7 6.2 %copy-start.6 = (f32[8,1024]{1,0:T(8,128)S(1)}, f32[8,1024]{1,0:T(8,128)}, u32[]{:S(2)}) copy-start(f32[8,1024]{1,0:T(8,128)} %param.23) | copy-start | bytes 98308
  375.7 6.8 %copy-start.2 = (bf16[8,1024,128]{2,1,0:T(8,128)(2,1)S(1)}, bf16[8,1024,128]{2,1,0:T(8,128)(2,1)}, u32[]{:S(2)}) copy-start(bf16[8,1024,128]{2,1,0:T(8,128)(2,1)} %get-tuple-element.209) | copy-start | bytes 6291460
  378.4 4.1 copy-start.1
Sparse Core Ops, SparseCore 0:
  224.7 148.0 reduce-scatter.1
  378.5 72.3 all-gather.1
where the time goes:
time: 463 us; the launch traced here: 462 us
  waiting for transfers between devices  252 us (54%)
  matrix products  118 us (25%)
  blocking collectives  41.2 us (9%)
  other arithmetic  15.1 us (3%)
  between operations  14.2 us (3%)
  starting transfers between devices  13.1 us (3%)
  local copies, waits for them, and re-layouts  8.86 us (2%)
    reduce_scatter x1, waiting for transfers between devices, per_device(): lax.psum_scatter(rem_grad, 'row', scatter_dimension=1, tiled=True)  148 us
    all_gather x1, waiting for transfers between devices, per_device(): rem_out = lax.all_gather(fresh_rows, 'row', axis=1, tiled=True)  66.2 us
    dot_general x8, matrix products, table_grads(): lax.dot_general(r_hot.astype(jnp.float32), grad_f * quot_pick, over_rows,...  49.6 us
    psum x1, blocking collectives, per_device(): rank_left, rank_right = lax.psum((rank_left, rank_right), 'table')  41.2 us
    all_to_all x1, waiting for transfers between devices, per_device(): lax.all_to_all(send_rows, 'row', split_axis=1, concat_axis=1, tiled=True)  37.7 us
    dot_general x8, matrix products, table_grads(): lax.dot_general(q_hot.astype(jnp.float32), grad_f * rem_pick, over_rows,...  28.4 us
    dot_general x8, matrix products, table_grads(): rem_pick = jnp.dot(r_hot, rtab, preferred_element_type=jnp.float32)  18.1 us
    dot_general x8, matrix products, table_grads(): quot_pick = jnp.dot(q_hot, slab, preferred_element_type=jnp.float32)  13.5 us
  transfers between devices with their start and end apart: 4, of which 3 were waited for; matrix products, arithmetic and copies ran while one was open for 3% of the time, Pallas kernels for 0%

commit v1 on v0

--- a/solution.py
+++ b/solution.py
@@ -1,42 +1,253 @@
+import functools
+
 import jax
 import jax.numpy as jnp
 from jax import lax
+from jax.experimental import pallas as pl
+from jax.experimental.pallas import tpu as pltpu
 from jax.sharding import PartitionSpec as P
 
 step_rate = 0.3
 epsilon = 1e-06
-
-
-def table_grads(items):
-    grads, keys, slab, rtab = items
-    rem_count = rtab.shape[0]
-    qlocal = keys // rem_count
-    rlocal = keys % rem_count
-    q_hot = (qlocal[:, None] == jnp.arange(slab.shape[0], dtype=jnp.int32)[None, :]).astype(
-        jnp.bfloat16
-    )
-    r_hot = (rlocal[:, None] == jnp.arange(rem_count, dtype=jnp.int32)[None, :]).astype(
-        jnp.bfloat16
-    )
-    rem_pick = jnp.dot(r_hot, rtab, preferred_element_type=jnp.float32)
-    quot_pick = jnp.dot(q_hot, slab, preferred_element_type=jnp.float32)
-    grad_f = grads.astype(jnp.float32)
-    over_rows = (((0,), (0,)), ((), ()))
-    grad_q = lax.dot_general(
-        q_hot.astype(jnp.float32),
-        grad_f * rem_pick,
-        over_rows,
-        precision=lax.Precision.HIGHEST,
-        preferred_element_type=jnp.float32,
-    )
-    grad_r = lax.dot_general(
-        r_hot.astype(jnp.float32),
-        grad_f * quot_pick,
-        over_rows,
-        precision=lax.Precision.HIGHEST,
-        preferred_element_type=jnp.float32,
-    )
-    return (grad_q, grad_r)
+MESH = pl.DeviceIdType.MESH
+
+
+def enter(axis, size):
+    me = lax.axis_index(axis)
+    barrier = pltpu.get_barrier_semaphore()
+    for hop in range(1, size):
+        pl.semaphore_signal(
+            barrier, inc=1, device_id={axis: lax.rem(me + hop, size)}, device_id_type=MESH
+        )
+    pl.semaphore_wait(barrier, size - 1)
+
+
+def digits(me, levels):
+    return [lax.rem(me // (1 << b), 2) for b in range(levels)]
+
+
+def across(me, bit, b):
+    return me + (1 - 2 * bit) * (1 << b)
+
+
+def one_hot(wanted, first, shape, axis):
+    names = lax.broadcasted_iota(jnp.int32, shape, axis) + first
+    return jnp.where(names == wanted, 1.0, 0.0).astype(jnp.bfloat16)
+
+
+def tables_kernel(
+    n,
+    levels,
+    send_ref,
+    cols_ref,
+    rows_ref,
+    slab_ref,
+    qacc_ref,
+    rem_ref,
+    racc_ref,
+    quot_ref,
+    qacc_out_ref,
+    rem_out_ref,
+    racc_out_ref,
+    got,
+    part,
+    *rest,
+):
+    held = list(rest[: levels - 1])
+    landed = list(rest[levels - 1 : 2 * levels - 1])
+    deal_send, deal_recv, send_sem, recv_sem = rest[2 * levels - 1 :]
+    me = lax.axis_index("row")
+    bits = digits(me, levels)
+    tables, _, capacity, width = send_ref.shape
+    slots = n * capacity
+    rem_rows = rem_ref.shape[1]
+    quot_rows = slab_ref.shape[1]
+    share = rem_rows // n
+    every = slice(None)
+    stages = [part] + held
+
+    def deal(t, hop):
+        return pltpu.make_async_remote_copy(
+            src_ref=send_ref.at[t, lax.rem(me + hop, n)],
+            dst_ref=got.at[t, me],
+            send_sem=deal_send.at[t, hop - 1],
+            recv_sem=deal_recv.at[t, hop - 1],
+            device_id={"row": lax.rem(me + hop, n)},
+            device_id_type=MESH,
+        )
+
+    def halve(t, b):
+        where = (t,) + (every,) * (levels - b - 1) + (1 - bits[b],)
+        return pltpu.make_async_remote_copy(
+            src_ref=stages[b].at[where],
+            dst_ref=landed[b].at[t],
+            send_sem=send_sem.at[b, t],
+            recv_sem=recv_sem.at[b, t],
+            device_id={"row": across(me, bits[b], b)},
+            device_id_type=MESH,
+        )
+
+    def spread(t, b):
+        where = (t,) + (every,) * (levels - b - 1) + tuple(bits[c] for c in range(b, -1, -1))
+        return pltpu.make_async_remote_copy(
+            src_ref=rem_out_ref.at[where],
+            dst_ref=rem_out_ref.at[where],
+            send_sem=send_sem.at[levels + b, t],
+            recv_sem=recv_sem.at[levels + b, t],
+            device_id={"row": across(me, bits[b], b)},
+            device_id_type=MESH,
+        )
+
+    enter("row", n)
+
+    def start_deal(t, carry):
+        for hop in range(1, n):
+            deal(t, hop).start()
+        return carry
+
+    lax.fori_loop(0, tables, start_deal, 0)
+
+    def pick(wanted, table_ref, t, count):
+        total = jnp.zeros((slots, width), jnp.float32)
+        chunk = min(count, 512)
+        for first in range(0, count, chunk):
+            hot = one_hot(wanted, first, (slots, chunk), 1)
+            total += jnp.dot(
+                hot, table_ref[t, pl.ds(first, chunk), :], preferred_element_type=jnp.float32
+            )
+        return total
+
+    def table_step(t):
+        got[t, me] = send_ref[t, me]
+        for hop in range(1, n):
+            deal(t, hop).wait_recv()
+        grads = got[t].reshape(slots, width).astype(jnp.float32)
+        cols = cols_ref[t]
+        rows = rows_ref[t]
+        quot_pick = pick(cols[:, 0:1], slab_ref, t, quot_rows)
+        for_rem = (grads * quot_pick).astype(jnp.bfloat16)
+        chunk = max(share, 512)
+        for first in range(0, rem_rows, chunk):
+            hot = one_hot(rows[1:2, :], first, (chunk, slots), 0)
+            grad = jnp.dot(hot, for_rem, preferred_element_type=jnp.float32)
+            for r in range(first // share, (first + chunk) // share):
+                where = tuple((r >> b) & 1 for b in range(levels - 1, -1, -1))
+                part[(t,) + where] = grad[r * share - first : (r + 1) * share - first].astype(
+                    jnp.bfloat16
+                )
+        halve(t, 0).start()
+        rem_pick = pick(cols[:, 1:2], rem_ref, t, rem_rows)
+        for_quot = (grads * rem_pick).astype(jnp.bfloat16)
+        chunk = min(quot_rows, 512)
+        for first in range(0, quot_rows, chunk):
+            here = pl.ds(first, chunk)
+            hot = one_hot(rows[0:1, :], first, (chunk, slots), 0)
+            grad = jnp.dot(hot, for_quot, preferred_element_type=jnp.float32)
+            fresh, fresh_acc = adagrad(slab_ref[t, here, :], qacc_ref[t, :, here], grad)
+            quot_ref[t, here, :] = fresh
+            qacc_out_ref[t, :, here] = fresh_acc
+
+    def adagrad(old, accum, grad):
+        count = old.shape[0]
+        mean = jnp.mean(grad * grad, axis=-1, keepdims=True)
+        fresh_acc = jnp.broadcast_to(accum, (width, count)).T + mean
+        fresh = old.astype(jnp.float32) - step_rate * grad * lax.rsqrt(fresh_acc + epsilon)
+        return fresh.astype(jnp.bfloat16), fresh_acc.T[0:1, :]
+
+    def sum_of(t, b, where):
+        kept = stages[b][(t,) + where + (bits[b],)].astype(jnp.float32)
+        return kept + landed[b][(t,) + where].astype(jnp.float32)
+
+    def comm_step(t, s):
+        if s <= levels:
+            halve(t, s - 1).wait_recv()
+            if s < levels:
+                for i in range(1 << (levels - s)):
+                    where = tuple((i >> b) & 1 for b in range(levels - s - 1, -1, -1))
+                    held[s - 1][(t,) + where] = sum_of(t, s - 1, where).astype(jnp.bfloat16)
+                halve(t, s).start()
+            else:
+                old = rem_ref[t, pl.ds(pl.multiple_of(me * share, share), share), :]
+                fresh, fresh_acc = adagrad(old, racc_ref[t], sum_of(t, s - 1, ()))
+                rem_out_ref[(t,) + tuple(bits[::-1])] = fresh
+                racc_out_ref[t] = fresh_acc
+                spread(t, levels - 1).start()
+        else:
+            b = 2 * levels - s
+            spread(t, b).wait_recv()
+            if b > 0:
+                spread(t, b - 1).start()
+
+    def step(i, carry):
+        @pl.when(i < tables)
+        def _():
+            table_step(i)
+
+        for s in range(2 * levels, 0, -1):
+            t = i - s
+
+            @pl.when((t >= 0) & (t < tables))
+            def _():
+                comm_step(t, s)
+
+        return carry
+
+    lax.fori_loop(0, tables + 2 * levels, step, 0)
+
+    def finish(t, carry):
+        for hop in range(1, n):
+            deal(t, hop).wait_send()
+        for b in range(levels):
+            halve(t, b).wait_send()
+            spread(t, b).wait_send()
+        return carry
+
+    lax.fori_loop(0, tables, finish, 0)
+
+
+def tables_call(send_rows, keys, slab, qacc, rem_table, rem_accum):
+    tables, n, capacity, width = send_rows.shape
+    levels = n.bit_length() - 1
+    rem_rows, quot_rows = rem_table.shape[1], slab.shape[1]
+    share = rem_rows // n
+    both = jnp.stack((keys // rem_rows, keys % rem_rows), axis=1)
+    own_acc = lax.dynamic_slice_in_dim(rem_accum, lax.axis_index("row") * share, share, 1)
+    vmem = pl.BlockSpec(memory_space=pltpu.VMEM)
+    cube = lambda b: (tables,) + (2,) * b + (share, width)
+    outs = pl.pallas_call(
+        functools.partial(tables_kernel, n, levels),
+        out_shape=(
+            jax.ShapeDtypeStruct(slab.shape, jnp.bfloat16),
+            jax.ShapeDtypeStruct((tables, 1, quot_rows), jnp.float32),
+            jax.ShapeDtypeStruct(cube(levels), jnp.bfloat16),
+            jax.ShapeDtypeStruct((tables, 1, share), jnp.float32),
+        ),
+        in_specs=[vmem] * 7,
+        out_specs=(vmem,) * 4,
+        scratch_shapes=[pltpu.VMEM((tables, n, capacity, width), jnp.bfloat16)]
+        + [pltpu.VMEM(cube(b), jnp.bfloat16) for b in range(levels, 0, -1)]
+        + [pltpu.VMEM(cube(b), jnp.bfloat16) for b in range(levels - 1, -1, -1)]
+        + [pltpu.SemaphoreType.DMA((tables, n - 1))] * 2
+        + [pltpu.SemaphoreType.DMA((2 * levels, tables))] * 2,
+        compiler_params=pltpu.CompilerParams(
+            collective_id=0, has_side_effects=True, vmem_limit_bytes=60 << 20
+        ),
+    )(
+        send_rows,
+        both.transpose(0, 2, 1),
+        both,
+        slab,
+        qacc[:, None, :],
+        rem_table,
+        own_acc[:, None, :],
+    )
+    quot_out, quot_acc_out, rem_out, rem_acc_out = outs
+    return (
+        quot_out,
+        quot_acc_out[:, 0],
+        rem_out.reshape(rem_table.shape),
+        rem_acc_out[:, 0],
+    )
 
 
 def per_device(
@@ -95,30 +306,9 @@
     send_keys = jnp.sum(jnp.where(placed, key_words[:, :, None], 0), axis=1)
     send_rows = send_rows.reshape(tables_dev, row_count, capacity, row_width)
     send_keys = send_keys.reshape(tables_dev, row_count, capacity)
-    got_rows, got_keys = (
-        lax.all_to_all(send_rows, "row", split_axis=1, concat_axis=1, tiled=True),
-        lax.all_to_all(send_keys, "row", split_axis=1, concat_axis=1, tiled=True),
-    )
-    got_rows = got_rows.reshape(tables_dev, slots, row_width)
+    got_keys = lax.all_to_all(send_keys, "row", split_axis=1, concat_axis=1, tiled=True)
     got_keys = got_keys.reshape(tables_dev, slots)
-    quot_grad, rem_grad = lax.map(table_grads, (got_rows, got_keys, quot_slab, rem_table))
-    quot_acc_out = quot_accum + jnp.mean(quot_grad * quot_grad, axis=-1)
-    quot_out = (
-        quot_slab.astype(jnp.float32)
-        - step_rate * quot_grad * lax.rsqrt(quot_acc_out + epsilon)[..., None]
-    ).astype(jnp.bfloat16)
-    share = rem_rows // row_count
-    start = lax.axis_index("row") * share
-    rem_part = lax.psum_scatter(rem_grad, "row", scatter_dimension=1, tiled=True)
-    old_rows = lax.dynamic_slice_in_dim(rem_table, start, share, 1)
-    old_accum = lax.dynamic_slice_in_dim(rem_accum, start, share, 1)
-    rem_acc_out = old_accum + jnp.mean(rem_part * rem_part, axis=-1)
-    fresh_rows = (
-        old_rows.astype(jnp.float32)
-        - step_rate * rem_part * lax.rsqrt(rem_acc_out + epsilon)[..., None]
-    ).astype(jnp.bfloat16)
-    rem_out = lax.all_gather(fresh_rows, "row", axis=1, tiled=True)
-    return (quot_out, quot_acc_out, rem_out, rem_acc_out)
+    return tables_call(send_rows, got_keys, quot_slab, quot_accum, rem_table, rem_accum)
 
 
 def solution(mesh):

time: 463 us -> 207 us (0.45)
  waiting for transfers between devices: 252 us -> 0.01 us
  Pallas kernels: 0 us -> 129 us
  matrix products: 118 us -> 9.42 us
  between operations: 14.2 us -> 0.81 us
  other arithmetic: 15.1 us -> 3.93 us
  starting transfers between devices: 13.1 us -> 7.28 us
  local copies, waits for them, and re-layouts: 8.86 us -> 13.7 us
    reduce_scatter x1 -> x0, waiting for transfers between devices: 148 us -> none  [per_device(): lax.psum_scatter(rem_grad, 'row', scatter_dimension=1, tiled=True)]
    pallas_call x0 -> x1, Pallas kernels: none -> 129 us  [tables_call(): pl.pallas_call(functools.partial(tables_kernel, n, levels), out_shape=(ja...]
    dot_general x32 -> x0, matrix products: 110 us -> none  [the longest x8 49.6 us: table_grads(): lax.dot_general(r_hot.astype(jnp.float32), grad_f * quot_pick, over_rows,...]
    all_gather x1 -> x0, waiting for transfers between devices: 66.2 us -> none  [per_device(): rem_out = lax.all_gather(fresh_rows, 'row', axis=1, tiled=True)]
    all_to_all x1 -> x0, waiting for transfers between devices: 37.7 us -> none  [per_device(): lax.all_to_all(send_rows, 'row', split_axis=1, concat_axis=1, tiled=True)]
    all_to_all x1 -> x0, starting transfers between devices: 5.31 us -> none  [per_device(): lax.all_to_all(send_rows, 'row', split_axis=1, concat_axis=1, tiled=True)]
    reduce_sum x2 -> x0, other arithmetic: 5.06 us -> none  [the longest x1 3.49 us: per_device(): quot_acc_out = quot_accum + jnp.mean(quot_grad * quot_grad, axis=-1)]
    convert_element_type x2 -> x0, other arithmetic: 4.89 us -> none  [the longest x1 2.67 us: per_device(): fresh_rows = (old_rows.astype(jnp.float32) - step_rate * rem_part * lax.r...]
  transfers between devices with their start and end apart: 4 -> 1, of which waited for: 3 -> 0; matrix products, arithmetic and copies ran while one was open for 3% -> 5% of each run, Pallas kernels for 0% -> 0%
where the time goes in v1:
time: 207 us; the launch traced here: 205 us
  Pallas kernels  129 us (62%)
  blocking collectives  41.4 us (20%)
  local copies, waits for them, and re-layouts  13.7 us (7%)
  matrix products  9.42 us (5%)
  starting transfers between devices  7.28 us (4%)
  other arithmetic  3.93 us (2%)
    pallas_call x1, Pallas kernels, tables_call(): pl.pallas_call(functools.partial(tables_kernel, n, levels), out_shape=(ja...  129 us
    psum x1, blocking collectives, per_device(): rank_left, rank_right = lax.psum((rank_left, rank_right), 'table')  41.4 us
    unnamed x24, local copies, waits for them, and re-layouts  8.76 us
    all_to_all x1, starting transfers between devices, per_device(): lax.all_to_all(send_keys, 'row', split_axis=1, concat_axis=1, tiled=True)  7.28 us
  transfers between devices with their start and end apart: 1, of which 0 were waited for; matrix products, arithmetic and copies ran while one was open for 5% of the time, Pallas kernels for 0%

profile of v1, /device:TPU:0, one launch (start us, length us, event | category | flops | bytes accessed | tf_op | source)
XLA Modules:
  0.0 205.3 jit_solution(2179267365888006995)
XLA Ops:
  0.6 0.0 copy-start
  0.6 0.8 copy.40
  1.5 0.3 fusion.8
  1.8 0.7 reshape_add_fusion
  2.5 0.7 multiply_add_fusion
  3.3 1.6 select_reduce_fusion
  4.9 0.1 reshape.142
  5.0 0.6 copy.22
  5.6 7.3 %all-to-all-start = ((s32[8,8,96]{2,0,1:T(8,128)}), s32[8,8,96]{2,0,1:T(8,128)S(1)}, u32[]{:S(2)}, u32[]{:S(2)}) async-start(s32[8,8,96]{2,0,1:T(8,128)} %copy.22), calls=%async_computation | async-start | bytes 65536 | tf_op jit(solution)/shard_map/all_to_all | solution.py:309
  12.9 0.0 copy-done
  12.9 0.0 copy-start.2
  12.9 0.0 copy-start.5
  12.9 2.4 %fusion.9 = f32[512,512]{1,0:T(8,128)S(1)} fusion(bf16[1024,512]{1,0:T(8,128)(2,1)S(1)} %copy-done, bf16[512,1024]{1,0:T(8,128)(2,1)} %param.13, bf16[512,1024]{1,0:T(8,128)(2,1)} %param.12), kind=kOutput, calls=%fused_computation.14 | convolution fusion | flops 538968064 | bytes 4194304 | tf_op jit(solution)/shard_map/dot_general | solution.py:277
  15.3 0.0 copy-done.2
  15.3 0.0 copy-done.5
  15.3 0.7 fusion.20
  16.0 41.4 %all-reduce.2 = (bf16[512,512]{1,0:T(8,128)(2,1)}, bf16[512,512]{1,0:T(8,128)(2,1)}) all-reduce(f32[512,512]{1,0:T(8,128)S(1)} %fusion.20, f32[512,512]{1,0:T(8,128)S(1)} %fusion.9), channel_id=1, replica_groups=mesh['table'=4,'row'=8] {'table'}, use_global_device_ids=true, to_apply=%region_1.0 | all-reduce | flops 524288 | bytes 3145728 | tf_op jit(solution)/shard_map/psum | solution.py:278
  57.4 0.0 copy-start.3
  57.4 0.0 copy-start.6
  57.4 0.0 copy-start.7
  57.4 0.0 copy-start.8
  57.4 1.9 fusion.21
  59.3 0.0 copy-done.3
  59.3 0.0 copy-done.6
  59.3 0.0 copy-done.7
  59.4 0.0 copy-done.8
  59.4 0.8 fusion.6
  60.2 0.0 copy-start.4
  60.2 3.3 %fusion.5 = bf16[8,768,128]{2,1,0:T(8,128)(2,1)} fusion(s32[8,512]{1,0:T(8,128)S(1)} %bitcast.40, bf16[64,8,8,128]{3,2,1,0:T(8,128)(2,1)S(1)} %fusion.6), kind=kOutput, calls=%fused_computation.9 | convolution fusion | flops 809238528 | bytes 2637824 | tf_op jit(solution)/shard_map/tsk,ste->tke/dot_general | solution.py:302
  63.5 0.7 constant_dynamic-slice_fusion
  64.2 0.6 broadcast_in_dim.33.racc_ref
  64.8 0.0 copy-done.4
  64.8 0.6 broadcast_in_dim.32.qacc_ref
  65.4 0.0 all-to-all-done
  65.4 0.1 reshape.143
  65.5 0.1 and_select_fusion.1
  65.7 0.7 pad_add_fusion
  66.4 2.2 %copy.24.cols_ref = s32[8,768,2]{2,1,0:T(8,128)} copy(s32[8,768,2]{1,2,0:T(2,128)S(1)} %get-tuple-element.17) | data formatting | bytes 98304 | tf_op jit(solution)/shard_map/transpose | solution.py:237
  68.6 128.9 %shard_map.147 = (bf16[8,1024,128]{2,1,0:T(8,128)(2,1)}, f32[8,1,1024]{2,1,0:T(1,128)}, bf16[8,2,2,2,256,128]{5,4,3,2,1,0:T(8,128)(2,1)}, f32[8,1,256]{2,1,0:T(1,128)}) custom-call(bf16[8,8,96,128]{3,2,1,0:T(8,128)(2,1)} %bitcast.38, s32[8,768,2]{2,1,0:T(8,128)} %copy.24.cols_ref, s32[8,2,768]{2,1,0:T(2,128)} %get-tuple-element.16.rows_ref, ...), custom_call_target="tpu_custom_call" | custom-call | tf_op jit(solution)/shard_map/pallas_call | solution.py:217
  197.4 1.3 copy.41
  198.7 1.4 copy.38
  200.1 0.0 copy-start.1
  200.1 3.2 %copy.48 = bf16[8,1024,128]{2,1,0:T(8,128)(2,1)} copy(bf16[8,1024,128]{2,1,0:T(8,128)(2,1)} %get-tuple-element.22) | data formatting | bytes 4194304
  203.3 0.0 copy-done.1
  203.3 2.0 copy.49
  (4 shorter events, 0.1 us)
Async XLA Ops:
  0.6 12.2 %copy-start = (bf16[1024,512]{1,0:T(8,128)(2,1)S(1)}, bf16[1024,512]{1,0:T(8,128)(2,1)}, u32[]{:S(2)}) copy-start(bf16[1024,512]{1,0:T(8,128)(2,1)} %param.15) | copy-start | bytes 3145732
  5.6 59.8 %all-to-all-start = ((s32[8,8,96]{2,0,1:T(8,128)}), s32[8,8,96]{2,0,1:T(8,128)S(1)}, u32[]{:S(2)}, u32[]{:S(2)}) async-start(s32[8,8,96]{2,0,1:T(8,128)} %copy.22), calls=%async_computation | async-start | bytes 65536 | tf_op jit(solution)/shard_map/all_to_all | solution.py:309
  12.9 2.4 %copy-start.2 = (bf16[512,1024]{1,0:T(8,128)(2,1)S(1)}, bf16[512,1024]{1,0:T(8,128)(2,1)}, u32[]{:S(2)}) copy-start(bf16[512,1024]{1,0:T(8,128)(2,1)} %param.12) | copy-start | bytes 3145732
  12.9 2.4 %copy-start.5 = (bf16[1024,512]{1,0:T(8,128)(2,1)S(1)}, bf16[1024,512]{1,0:T(8,128)(2,1)}, u32[]{:S(2)}) copy-start(bf16[1024,512]{1,0:T(8,128)(2,1)} %param.14) | copy-start | bytes 3145732
  57.4 1.9 copy-start.3
  57.4 1.9 copy-start.6
  57.4 2.0 copy-start.7
  57.4 2.0 copy-start.8
  60.2 4.6 %copy-start.4 = (f32[8,1024]{1,0:T(8,128)S(1)}, f32[8,1024]{1,0:T(8,128)}, u32[]{:S(2)}) copy-start(f32[8,1024]{1,0:T(8,128)} %param.21) | copy-start | bytes 98308
  200.1 3.2 %copy-start.1 = (bf16[8,2,2,2,256,128]{5,4,3,2,1,0:T(8,128)(2,1)S(1)}, bf16[8,2,2,2,256,128]{5,4,3,2,1,0:T(8,128)(2,1)}, u32[]{:S(2)}) copy-start(bf16[8,2,2,2,256,128]{5,4,3,2,1,0:T(8,128)(2,1)} %get-tuple-element.10) | copy-start | bytes 12582916

commit v2 on v1

--- a/solution.py
+++ b/solution.py
@@ -39,7 +39,6 @@
     n,
     levels,
     send_ref,
-    cols_ref,
     rows_ref,
     slab_ref,
     qacc_ref,
@@ -122,9 +121,9 @@
         for hop in range(1, n):
             deal(t, hop).wait_recv()
         grads = got[t].reshape(slots, width).astype(jnp.float32)
-        cols = cols_ref[t]
         rows = rows_ref[t]
-        quot_pick = pick(cols[:, 0:1], slab_ref, t, quot_rows)
+        cols = [jnp.broadcast_to(rows[i : i + 1, :], (width, slots)).T[:, 0:1] for i in range(2)]
+        quot_pick = pick(cols[0], slab_ref, t, quot_rows)
         for_rem = (grads * quot_pick).astype(jnp.bfloat16)
         chunk = max(share, 512)
         for first in range(0, rem_rows, chunk):
@@ -136,7 +135,7 @@
                     jnp.bfloat16
                 )
         halve(t, 0).start()
-        rem_pick = pick(cols[:, 1:2], rem_ref, t, rem_rows)
+        rem_pick = pick(cols[1], rem_ref, t, rem_rows)
         for_quot = (grads * rem_pick).astype(jnp.bfloat16)
         chunk = min(quot_rows, 512)
         for first in range(0, quot_rows, chunk):
@@ -167,8 +166,9 @@
                     held[s - 1][(t,) + where] = sum_of(t, s - 1, where).astype(jnp.bfloat16)
                 halve(t, s).start()
             else:
-                old = rem_ref[t, pl.ds(pl.multiple_of(me * share, share), share), :]
-                fresh, fresh_acc = adagrad(old, racc_ref[t], sum_of(t, s - 1, ()))
+                mine = pl.ds(pl.multiple_of(me * share, share), share)
+                accum = racc_ref[t, :, mine]
+                fresh, fresh_acc = adagrad(rem_ref[t, mine, :], accum, sum_of(t, s - 1, ()))
                 rem_out_ref[(t,) + tuple(bits[::-1])] = fresh
                 racc_out_ref[t] = fresh_acc
                 spread(t, levels - 1).start()
@@ -211,7 +211,6 @@
     rem_rows, quot_rows = rem_table.shape[1], slab.shape[1]
     share = rem_rows // n
     both = jnp.stack((keys // rem_rows, keys % rem_rows), axis=1)
-    own_acc = lax.dynamic_slice_in_dim(rem_accum, lax.axis_index("row") * share, share, 1)
     vmem = pl.BlockSpec(memory_space=pltpu.VMEM)
     cube = lambda b: (tables,) + (2,) * b + (share, width)
     outs = pl.pallas_call(
@@ -222,7 +221,7 @@
             jax.ShapeDtypeStruct(cube(levels), jnp.bfloat16),
             jax.ShapeDtypeStruct((tables, 1, share), jnp.float32),
         ),
-        in_specs=[vmem] * 7,
+        in_specs=[vmem] * 6,
         out_specs=(vmem,) * 4,
         scratch_shapes=[pltpu.VMEM((tables, n, capacity, width), jnp.bfloat16)]
         + [pltpu.VMEM(cube(b), jnp.bfloat16) for b in range(levels, 0, -1)]
@@ -234,12 +233,11 @@
         ),
     )(
         send_rows,
-        both.transpose(0, 2, 1),
         both,
         slab,
         qacc[:, None, :],
         rem_table,
-        own_acc[:, None, :],
+        rem_accum[:, None, :],
     )
     quot_out, quot_acc_out, rem_out, rem_acc_out = outs
     return (
@@ -248,6 +246,145 @@
         rem_out.reshape(rem_table.shape),
         rem_acc_out[:, 0],
     )
+
+
+def rank_kernel(
+    n_row,
+    n,
+    levels,
+    feats_ref,
+    cotan_ref,
+    in_ref,
+    out_ref,
+    bias_ref,
+    keys_ref,
+    pooled_ref,
+    got_ref,
+    part,
+    full,
+    *rest,
+):
+    held = list(rest[: levels - 1])
+    landed = list(rest[levels - 1 : 2 * levels - 1])
+    deal_send, deal_recv, send_sem, recv_sem = rest[2 * levels - 1 :]
+    row = lax.axis_index("row")
+    me = lax.axis_index("table")
+    bits = digits(me, levels)
+    every = slice(None)
+    stages = [part] + held
+    samples = feats_ref.shape[0]
+    rank = in_ref.shape[1]
+    share = samples // n
+
+    def deal(hop):
+        return pltpu.make_async_remote_copy(
+            src_ref=keys_ref.at[lax.rem(row + hop, n_row)],
+            dst_ref=got_ref.at[row],
+            send_sem=deal_send.at[hop - 1],
+            recv_sem=deal_recv.at[hop - 1],
+            device_id={"row": lax.rem(row + hop, n_row)},
+            device_id_type=MESH,
+        )
+
+    def halve(t, b):
+        where = (t,) + (every,) * (levels - b - 1) + (1 - bits[b],)
+        return pltpu.make_async_remote_copy(
+            src_ref=stages[b].at[where],
+            dst_ref=landed[b].at[t],
+            send_sem=send_sem.at[b, t],
+            recv_sem=recv_sem.at[b, t],
+            device_id={"table": across(me, bits[b], b)},
+            device_id_type=MESH,
+        )
+
+    def spread(t, b):
+        where = (t,) + (every,) * (levels - b - 1) + tuple(bits[c] for c in range(b, -1, -1))
+        return pltpu.make_async_remote_copy(
+            src_ref=full.at[where],
+            dst_ref=full.at[where],
+            send_sem=send_sem.at[levels + b, t],
+            recv_sem=recv_sem.at[levels + b, t],
+            device_id={"table": across(me, bits[b], b)},
+            device_id_type=MESH,
+        )
+
+    barrier = pltpu.get_barrier_semaphore()
+    for axis, size, at in (("table", n, me), ("row", n_row, row)):
+        for hop in range(1, size):
+            pl.semaphore_signal(
+                barrier, inc=1, device_id={axis: lax.rem(at + hop, size)}, device_id_type=MESH
+            )
+    pl.semaphore_wait(barrier, n + n_row - 2)
+    for hop in range(1, n_row):
+        deal(hop).start()
+
+    def project(t, source, weight_ref):
+        partial = jnp.dot(source, weight_ref[...], preferred_element_type=jnp.float32)
+        part[t] = partial.astype(jnp.bfloat16).reshape(part.shape[1:])
+        halve(t, 0).start()
+
+    feats = feats_ref[...]
+    cotan = cotan_ref[...].astype(jnp.float32)
+    project(0, feats, in_ref)
+    project(1, (cotan * feats.astype(jnp.float32)).astype(jnp.bfloat16), out_ref)
+    got_ref[row] = keys_ref[row]
+    for b in range(levels):
+        for t in range(2):
+            halve(t, b).wait_recv()
+            mine = stages[b][(t,) + (every,) * (levels - b - 1) + (bits[b],)].astype(jnp.float32)
+            total = (mine + landed[b][t].astype(jnp.float32)).astype(jnp.bfloat16)
+            if b < levels - 1:
+                held[b][t] = total
+                halve(t, b + 1).start()
+            else:
+                full[(t,) + tuple(bits[::-1])] = total
+                spread(t, b).start()
+    for b in range(levels - 1, 0, -1):
+        for t in range(2):
+            spread(t, b).wait_recv()
+            spread(t, b - 1).start()
+    contract = (((1,), (1,)), ((), ()))
+    back = []
+    for t, weight_ref in ((0, out_ref), (1, in_ref)):
+        spread(t, 0).wait_recv()
+        whole = full[t].reshape(samples, rank)
+        back.append(
+            lax.dot_general(whole, weight_ref[...], contract, preferred_element_type=jnp.float32)
+        )
+    pooled = cotan * (back[0] + bias_ref[...] + 1.0) + back[1]
+    pooled_ref[...] = pooled.astype(jnp.bfloat16)
+    for hop in range(1, n_row):
+        deal(hop).wait()
+    for t in range(2):
+        for b in range(levels):
+            halve(t, b).wait_send()
+            spread(t, b).wait_send()
+
+
+def rank_call(features, cotangent, cross_in, cross_out, bias, keys):
+    n_row, n = lax.axis_size("row"), lax.axis_size("table")
+    levels = n.bit_length() - 1
+    samples, columns = features.shape
+    share, rank = samples // n, cross_in.shape[1]
+    vmem = pl.BlockSpec(memory_space=pltpu.VMEM)
+    cube = lambda b: pltpu.VMEM((2,) + (2,) * b + (share, rank), jnp.bfloat16)
+    return pl.pallas_call(
+        functools.partial(rank_kernel, n_row, n, levels),
+        out_shape=(
+            jax.ShapeDtypeStruct((samples, columns), jnp.bfloat16),
+            jax.ShapeDtypeStruct(keys.shape, jnp.int32),
+        ),
+        in_specs=[vmem] * 6,
+        out_specs=(vmem,) * 2,
+        scratch_shapes=[cube(levels), cube(levels)]
+        + [cube(b) for b in range(levels - 1, 0, -1)]
+        + [cube(b) for b in range(levels - 1, -1, -1)]
+        + [pltpu.SemaphoreType.DMA((n_row - 1,))] * 2
+        + [pltpu.SemaphoreType.DMA((2 * levels, 2))] * 2,
+        compiler_params=pltpu.CompilerParams(
+            collective_id=1, has_side_effects=True, vmem_limit_bytes=60 << 20
+        ),
+    )(features, cotangent, cross_in, cross_out, bias[None, :], keys)
 
 
 def per_device(
@@ -264,7 +401,6 @@
     rem_table,
     rem_accum,
 ):
-    contract = (((1,), (1,)), ((), ()))
     samples = features.shape[0]
     tables_dev = quot_slab.shape[0]
     row_width = quot_slab.shape[2]
@@ -272,21 +408,6 @@
     row_count = lax.axis_size("row")
     capacity = 3 * samples // (2 * row_count)
     slots = row_count * capacity
-    product = (cotangent.astype(jnp.float32) * features.astype(jnp.float32)).astype(jnp.bfloat16)
-    rank_left = jnp.dot(features, cross_in, preferred_element_type=jnp.float32)
-    rank_right = jnp.dot(product, cross_out, preferred_element_type=jnp.float32)
-    rank_left, rank_right = lax.psum((rank_left, rank_right), "table")
-    cross_gate = (
-        lax.dot_general(
-            rank_left.astype(jnp.bfloat16), cross_out, contract, preferred_element_type=jnp.float32
-        )
-        + bias
-    )
-    cross_back = lax.dot_general(
-        rank_right.astype(jnp.bfloat16), cross_in, contract, preferred_element_type=jnp.float32
-    )
-    pooled = (cotangent.astype(jnp.float32) * (cross_gate + 1.0) + cross_back).astype(jnp.bfloat16)
-    pooled = pooled.reshape(samples, tables_dev, row_width)
     target = dest_shard[:, :, 0]
     onehot = target[:, :, None] == jnp.arange(row_count, dtype=jnp.int32)[None, None, :]
     lower = (
@@ -299,15 +420,16 @@
     slot_index = jnp.sum(jnp.where(onehot, running, 0.0), axis=2).astype(jnp.int32) - 1
     position = target * capacity + slot_index
     placed = position[:, :, None] == jnp.arange(slots, dtype=jnp.int32)[None, None, :]
+    key_words = quot_row * rem_rows + rem_row
+    send_keys = jnp.sum(jnp.where(placed, key_words[:, :, None], 0), axis=1)
+    send_keys = send_keys.reshape(tables_dev, row_count, capacity).transpose(1, 0, 2)
+    pooled, got_keys = rank_call(features, cotangent, cross_in, cross_out, bias, send_keys)
+    pooled = pooled.reshape(samples, tables_dev, row_width)
     send_rows = jnp.einsum(
         "tsk,ste->tke", placed.astype(jnp.bfloat16), pooled, preferred_element_type=jnp.float32
     ).astype(jnp.bfloat16)
-    key_words = quot_row * rem_rows + rem_row
-    send_keys = jnp.sum(jnp.where(placed, key_words[:, :, None], 0), axis=1)
     send_rows = send_rows.reshape(tables_dev, row_count, capacity, row_width)
-    send_keys = send_keys.reshape(tables_dev, row_count, capacity)
-    got_keys = lax.all_to_all(send_keys, "row", split_axis=1, concat_axis=1, tiled=True)
-    got_keys = got_keys.reshape(tables_dev, slots)
+    got_keys = got_keys.transpose(1, 0, 2).reshape(tables_dev, slots)
     return tables_call(send_rows, got_keys, quot_slab, quot_accum, rem_table, rem_accum)
 
 

time: 207 us -> 178 us (0.86)
  blocking collectives: 41.4 us -> 0 us
  Pallas kernels: 129 us -> 155 us
  starting transfers between devices: 7.28 us -> 0 us
  matrix products: 9.42 us -> 4.84 us
    psum x1 -> x0, blocking collectives: 41.4 us -> none  [per_device(): rank_left, rank_right = lax.psum((rank_left, rank_right), 'table')]
    pallas_call x0 -> x1, Pallas kernels: none -> 27.7 us  [rank_call(): pl.pallas_call(functools.partial(rank_kernel, n_row, n, levels), out_shap...]
    all_to_all x1 -> x0, starting transfers between devices: 7.28 us -> none  [per_device(): lax.all_to_all(send_keys, 'row', split_axis=1, concat_axis=1, tiled=True)]
    dot_general x4 -> x0, matrix products: 5.82 us -> none  [the longest x1 2.4 us: per_device(): rank_right = jnp.dot(product, cross_out, preferred_element_type=jnp.float32)]
    unnamed x24 -> x8, local copies, waits for them, and re-layouts: 8.76 us -> 8.62 us
  transfers between devices with their start and end apart: 1 -> 0, of which waited for: 0 -> 0; matrix products, arithmetic and copies ran while one was open for 5% -> 0% of each run, Pallas kernels for 0% -> 0%
where the time goes in v2:
time: 178 us; the launch traced here: 177 us
  Pallas kernels  155 us (87%)
  local copies, waits for them, and re-layouts  13.1 us (7%)
  matrix products  4.84 us (3%)
  other arithmetic  3.91 us (2%)
    pallas_call x1, Pallas kernels, tables_call(): pl.pallas_call(functools.partial(tables_kernel, n, levels), out_shape=(ja...  127 us
    pallas_call x1, Pallas kernels, rank_call(): pl.pallas_call(functools.partial(rank_kernel, n_row, n, levels), out_shap...  27.7 us
    unnamed x8, local copies, waits for them, and re-layouts  8.62 us
    dot_general x1, matrix products, per_device(): jnp.einsum('tsk,ste->tke', placed.astype(jnp.bfloat16), pooled, preferred...  4.56 us

profile of v2, /device:TPU:0, one launch (start us, length us, event | category | flops | bytes accessed | tf_op | source)
XLA Modules:
  0.0 177.3 jit_solution(15742596470961364325)
XLA Ops:
  0.6 0.7 multiply_add_fusion
  1.4 0.7 copy.38
  2.1 0.3 fusion.4
  2.4 0.7 reshape_add_fusion
  3.2 1.6 select_reduce_fusion
  4.8 0.1 reshape.139
  4.9 0.6 copy.36
  5.5 1.4 broadcast_in_dim.35.qacc_ref
  6.9 1.5 broadcast_in_dim.36.racc_ref
  8.4 27.7 %shard_map.147 = (bf16[512,1024]{1,0:T(8,128)(2,1)}, s32[8,8,96]{2,1,0:T(8,128)}) custom-call(bf16[512,1024]{1,0:T(8,128)(2,1)} %feats_ref.1, bf16[512,1024]{1,0:T(8,128)(2,1)} %cotan_ref.1, bf16[1024,512]{1,0:T(8,128)(2,1)} %in_ref.1, bf16[1024,512]{1,0:T(8,128)(2,1)} %out_ref.1, f32[1,1024]{1,0:T(1,128)} %bitcast.44, s32[8,8,96]{2,1,0:T(8,128)} %bitcast.37), custom_call_target="tpu_custom_call" | custom-call | tf_op jit(solution)/shard_map/pallas_call | solution.py:371
  36.1 0.8 copy.20
  36.8 0.1 reshape.142
  36.9 0.1 and_select_fusion.1
  37.1 0.7 pad_add_fusion.rows_ref
  37.8 4.6 %fusion.2 = bf16[8,768,128]{2,1,0:T(8,128)(2,1)} fusion(s32[8,512]{1,0:T(8,128)S(1)} %bitcast.39, bf16[512,1024]{1,0:T(8,128)(2,1)} %get-tuple-element.10), kind=kOutput, calls=%fused_computation.4 | convolution fusion | flops 809238528 | bytes 2637824 | tf_op jit(solution)/shard_map/tsk,ste->tke/dot_general | solution.py:428
  42.3 127.0 %shard_map.148 = (bf16[8,1024,128]{2,1,0:T(8,128)(2,1)}, f32[8,1,1024]{2,1,0:T(1,128)}, bf16[8,2,2,2,256,128]{5,4,3,2,1,0:T(8,128)(2,1)}, f32[8,1,256]{2,1,0:T(1,128)}) custom-call(bf16[8,8,96,128]{3,2,1,0:T(8,128)(2,1)} %bitcast.36, s32[8,2,768]{2,1,0:T(2,128)} %pad_add_fusion.rows_ref, bf16[8,1024,128]{2,1,0:T(8,128)(2,1)} %slab_ref.1, ...), custom_call_target="tpu_custom_call" | custom-call | tf_op jit(solution)/shard_map/pallas_call | solution.py:216
  169.4 0.0 copy-start
  169.4 1.4 copy.39
  170.8 1.4 copy.35
  172.2 3.1 %copy.42 = bf16[8,1024,128]{2,1,0:T(8,128)(2,1)} copy(bf16[8,1024,128]{2,1,0:T(8,128)(2,1)} %get-tuple-element.22) | data formatting | bytes 4194304
  175.3 0.0 copy-done
  175.3 2.0 %copy.43 = bf16[8,2048,128]{2,1,0:T(8,128)(2,1)} copy(bf16[8,2048,128]{2,1,0:T(8,128)(2,1)S(1)} %bitcast.35) | data formatting | bytes 8388608
  (3 shorter events, 0.0 us)
Async XLA Ops:
  169.4 5.9 %copy-start = (bf16[8,2,2,2,256,128]{5,4,3,2,1,0:T(8,128)(2,1)S(1)}, bf16[8,2,2,2,256,128]{5,4,3,2,1,0:T(8,128)(2,1)}, u32[]{:S(2)}) copy-start(bf16[8,2,2,2,256,128]{5,4,3,2,1,0:T(8,128)(2,1)} %get-tuple-element.14) | copy-start | bytes 12582916

commit v3 on v2

--- a/solution.py
+++ b/solution.py
@@ -49,12 +49,13 @@
     rem_out_ref,
     racc_out_ref,
     got,
-    part,
+    rem_keys,
+    products,
     *rest,
 ):
     held = list(rest[: levels - 1])
-    landed = list(rest[levels - 1 : 2 * levels - 1])
-    deal_send, deal_recv, send_sem, recv_sem = rest[2 * levels - 1 :]
+    landed = list(rest[levels - 1 : 2 * levels - 2])
+    key_send, key_recv, deal_send, deal_recv, send_sem, recv_sem = rest[2 * levels - 2 :]
     me = lax.axis_index("row")
     bits = digits(me, levels)
     tables, _, capacity, width = send_ref.shape
@@ -63,7 +64,8 @@
     quot_rows = slab_ref.shape[1]
     share = rem_rows // n
     every = slice(None)
-    stages = [part] + held
+    down = list(range(levels - 1, -1, -1))
+    orders = (tuple(down), tuple(down[:-2] + [0, 1]))
 
     def deal(t, hop):
         return pltpu.make_async_remote_copy(
@@ -75,27 +77,56 @@
             device_id_type=MESH,
         )
 
+    def swap_keys():
+        return pltpu.make_async_remote_copy(
+            src_ref=rem_keys.at[bits[0]],
+            dst_ref=rem_keys.at[bits[0]],
+            send_sem=key_send,
+            recv_sem=key_recv,
+            device_id={"row": across(me, bits[0], 0)},
+            device_id_type=MESH,
+        )
+
+    def swap(t):
+        return pltpu.make_async_remote_copy(
+            src_ref=products.at[t, bits[0]],
+            dst_ref=products.at[t, bits[0]],
+            send_sem=send_sem.at[0, t],
+            recv_sem=recv_sem.at[0, t],
+            device_id={"row": across(me, bits[0], 0)},
+            device_id_type=MESH,
+        )
+
     def halve(t, b):
         where = (t,) + (every,) * (levels - b - 1) + (1 - bits[b],)
         return pltpu.make_async_remote_copy(
-            src_ref=stages[b].at[where],
-            dst_ref=landed[b].at[t],
+            src_ref=held[b - 1].at[where],
+            dst_ref=landed[b - 1].at[t],
             send_sem=send_sem.at[b, t],
             recv_sem=recv_sem.at[b, t],
             device_id={"row": across(me, bits[b], b)},
             device_id_type=MESH,
         )
 
-    def spread(t, b):
-        where = (t,) + (every,) * (levels - b - 1) + tuple(bits[c] for c in range(b, -1, -1))
+    def spread(t, j, order):
+        done, b = order[:j], order[j]
+        where = (t,) + tuple(every if c in done else bits[c] for c in down)
         return pltpu.make_async_remote_copy(
             src_ref=rem_out_ref.at[where],
             dst_ref=rem_out_ref.at[where],
-            send_sem=send_sem.at[levels + b, t],
-            recv_sem=recv_sem.at[levels + b, t],
+            send_sem=send_sem.at[levels + j, t],
+            recv_sem=recv_sem.at[levels + j, t],
             device_id={"row": across(me, bits[b], b)},
             device_id_type=MESH,
         )
+
+    def by_order(t, act):
+        last = lax.rem(t, 4) == 3
+        for order, chosen in zip(orders, (jnp.logical_not(last), last)):
+
+            @pl.when(chosen)
+            def _():
+                act(order)
 
     enter("row", n)
 
@@ -105,6 +136,8 @@
         return carry
 
     lax.fori_loop(0, tables, start_deal, 0)
+    rem_keys[bits[0]] = rows_ref[:, 1:2, :]
+    swap_keys().start()
 
     def pick(wanted, table_ref, t, count):
         total = jnp.zeros((slots, width), jnp.float32)
@@ -125,16 +158,8 @@
         cols = [jnp.broadcast_to(rows[i : i + 1, :], (width, slots)).T[:, 0:1] for i in range(2)]
         quot_pick = pick(cols[0], slab_ref, t, quot_rows)
         for_rem = (grads * quot_pick).astype(jnp.bfloat16)
-        chunk = max(share, 512)
-        for first in range(0, rem_rows, chunk):
-            hot = one_hot(rows[1:2, :], first, (chunk, slots), 0)
-            grad = jnp.dot(hot, for_rem, preferred_element_type=jnp.float32)
-            for r in range(first // share, (first + chunk) // share):
-                where = tuple((r >> b) & 1 for b in range(levels - 1, -1, -1))
-                part[(t,) + where] = grad[r * share - first : (r + 1) * share - first].astype(
-                    jnp.bfloat16
-                )
-        halve(t, 0).start()
+        products[t, bits[0]] = for_rem
+        swap(t).start()
         rem_pick = pick(cols[1], rem_ref, t, rem_rows)
         for_quot = (grads * rem_pick).astype(jnp.bfloat16)
         chunk = min(quot_rows, 512)
@@ -154,11 +179,28 @@
         return fresh.astype(jnp.bfloat16), fresh_acc.T[0:1, :]
 
     def sum_of(t, b, where):
-        kept = stages[b][(t,) + where + (bits[b],)].astype(jnp.float32)
-        return kept + landed[b][(t,) + where].astype(jnp.float32)
+        kept = held[b - 1][(t,) + where + (bits[b],)].astype(jnp.float32)
+        return kept + landed[b - 1][(t,) + where].astype(jnp.float32)
+
+    def half_grad(t):
+        for j in range(0, n // 2, 2):
+            near = lax.broadcasted_iota(jnp.int32, (2 * share, slots), 0)
+            names = near + jnp.where(near >= share, share, 0) + (2 * j + bits[0]) * share
+            grad = jnp.zeros((2 * share, width), jnp.float32)
+            for side in range(2):
+                hot = jnp.where(names == rem_keys[side, t], 1.0, 0.0).astype(jnp.bfloat16)
+                grad += jnp.dot(hot, products[t, side], preferred_element_type=jnp.float32)
+            for i in range(2):
+                where = tuple(((j + i) >> b) & 1 for b in range(levels - 2, -1, -1))
+                held[0][(t,) + where] = grad[i * share : (i + 1) * share].astype(jnp.bfloat16)
 
     def comm_step(t, s):
-        if s <= levels:
+        if s == 1:
+            pl.when(t == 0)(lambda: swap_keys().wait_recv())
+            swap(t).wait_recv()
+            half_grad(t)
+            halve(t, 1).start()
+        elif s <= levels:
             halve(t, s - 1).wait_recv()
             if s < levels:
                 for i in range(1 << (levels - s)):
@@ -171,12 +213,16 @@
                 fresh, fresh_acc = adagrad(rem_ref[t, mine, :], accum, sum_of(t, s - 1, ()))
                 rem_out_ref[(t,) + tuple(bits[::-1])] = fresh
                 racc_out_ref[t] = fresh_acc
-                spread(t, levels - 1).start()
+                by_order(t, lambda order: spread(t, 0, order).start())
         else:
-            b = 2 * levels - s
-            spread(t, b).wait_recv()
-            if b > 0:
-                spread(t, b - 1).start()
+            j = s - levels - 1
+
+            def pass_on(order):
+                spread(t, j, order).wait_recv()
+                if j < levels - 1:
+                    spread(t, j + 1, order).start()
+
+            by_order(t, pass_on)
 
     def step(i, carry):
         @pl.when(i < tables)
@@ -197,12 +243,19 @@
     def finish(t, carry):
         for hop in range(1, n):
             deal(t, hop).wait_send()
-        for b in range(levels):
+        swap(t).wait_send()
+        for b in range(1, levels):
             halve(t, b).wait_send()
-            spread(t, b).wait_send()
+
+        def sent(order):
+            for j in range(levels):
+                spread(t, j, order).wait_send()
+
+        by_order(t, sent)
         return carry
 
     lax.fori_loop(0, tables, finish, 0)
+    swap_keys().wait_send()
 
 
 def tables_call(send_rows, keys, slab, qacc, rem_table, rem_accum):
@@ -224,8 +277,13 @@
         in_specs=[vmem] * 6,
         out_specs=(vmem,) * 4,
         scratch_shapes=[pltpu.VMEM((tables, n, capacity, width), jnp.bfloat16)]
-        + [pltpu.VMEM(cube(b), jnp.bfloat16) for b in range(levels, 0, -1)]
-        + [pltpu.VMEM(cube(b), jnp.bfloat16) for b in range(levels - 1, -1, -1)]
+        + [
+            pltpu.VMEM((2, tables, 1, n * capacity), jnp.int32),
+            pltpu.VMEM((tables, 2, n * capacity, width), jnp.bfloat16),
+        ]
+        + [pltpu.VMEM(cube(b), jnp.bfloat16) for b in range(levels - 1, 0, -1)]
+        + [pltpu.VMEM(cube(b), jnp.bfloat16) for b in range(levels - 2, -1, -1)]
+        + [pltpu.SemaphoreType.DMA(())] * 2
         + [pltpu.SemaphoreType.DMA((tables, n - 1))] * 2
         + [pltpu.SemaphoreType.DMA((2 * levels, tables))] * 2,
         compiler_params=pltpu.CompilerParams(

time: 178 us -> 181 us (1.017)
  Pallas kernels: 155 us -> 157 us
    pallas_call x1, Pallas kernels: 127 us -> 129 us  [tables_call(): pl.pallas_call(functools.partial(tables_kernel, n, levels), out_shape=(ja...]
where the time goes in v3:
time: 181 us; the launch traced here: 179 us
  Pallas kernels  157 us (87%)
  local copies, waits for them, and re-layouts  13.1 us (7%)
  matrix products  4.84 us (3%)
  other arithmetic  3.91 us (2%)
    pallas_call x1, Pallas kernels, tables_call(): pl.pallas_call(functools.partial(tables_kernel, n, levels), out_shape=(ja...  129 us
    pallas_call x1, Pallas kernels, rank_call(): pl.pallas_call(functools.partial(rank_kernel, n_row, n, levels), out_shap...  27.7 us
    unnamed x8, local copies, waits for them, and re-layouts  8.62 us
    dot_general x1, matrix products, per_device(): jnp.einsum('tsk,ste->tke', placed.astype(jnp.bfloat16), pooled, preferred...  4.56 us

profile of v3, /device:TPU:0, one launch (start us, length us, event | category | flops | bytes accessed | tf_op | source)
XLA Modules:
  0.0 179.4 jit_solution(8685847138541043115)
XLA Ops:
  0.6 0.7 multiply_add_fusion
  1.4 0.7 copy.38
  2.1 0.3 fusion.4
  2.4 0.7 reshape_add_fusion
  3.2 1.6 select_reduce_fusion
  4.8 0.1 reshape.139
  4.9 0.6 copy.36
  5.5 1.4 broadcast_in_dim.35.qacc_ref
  6.9 1.5 broadcast_in_dim.36.racc_ref
  8.4 27.7 %shard_map.147 = (bf16[512,1024]{1,0:T(8,128)(2,1)}, s32[8,8,96]{2,1,0:T(8,128)}) custom-call(bf16[512,1024]{1,0:T(8,128)(2,1)} %feats_ref.1, bf16[512,1024]{1,0:T(8,128)(2,1)} %cotan_ref.1, bf16[1024,512]{1,0:T(8,128)(2,1)} %in_ref.1, bf16[1024,512]{1,0:T(8,128)(2,1)} %out_ref.1, f32[1,1024]{1,0:T(1,128)} %bitcast.44, s32[8,8,96]{2,1,0:T(8,128)} %bitcast.37), custom_call_target="tpu_custom_call" | custom-call | tf_op jit(solution)/shard_map/pallas_call | solution.py:429
  36.1 0.8 copy.20
  36.8 0.1 reshape.142
  36.9 0.1 and_select_fusion.1
  37.1 0.7 pad_add_fusion.rows_ref
  37.8 4.6 %fusion.2 = bf16[8,768,128]{2,1,0:T(8,128)(2,1)} fusion(s32[8,512]{1,0:T(8,128)S(1)} %bitcast.39, bf16[512,1024]{1,0:T(8,128)(2,1)} %get-tuple-element.10), kind=kOutput, calls=%fused_computation.4 | convolution fusion | flops 809238528 | bytes 2637824 | tf_op jit(solution)/shard_map/tsk,ste->tke/dot_general | solution.py:486
  42.3 129.2 %shard_map.148 = (bf16[8,1024,128]{2,1,0:T(8,128)(2,1)}, f32[8,1,1024]{2,1,0:T(1,128)}, bf16[8,2,2,2,256,128]{5,4,3,2,1,0:T(8,128)(2,1)}, f32[8,1,256]{2,1,0:T(1,128)}) custom-call(bf16[8,8,96,128]{3,2,1,0:T(8,128)(2,1)} %bitcast.36, s32[8,2,768]{2,1,0:T(2,128)} %pad_add_fusion.rows_ref, bf16[8,1024,128]{2,1,0:T(8,128)(2,1)} %slab_ref.1, ...), custom_call_target="tpu_custom_call" | custom-call | tf_op jit(solution)/shard_map/pallas_call | solution.py:269
  171.5 0.0 copy-start
  171.5 1.4 copy.39
  173.0 1.4 copy.35
  174.4 3.1 %copy.42 = bf16[8,1024,128]{2,1,0:T(8,128)(2,1)} copy(bf16[8,1024,128]{2,1,0:T(8,128)(2,1)} %get-tuple-element.22) | data formatting | bytes 4194304
  177.4 0.0 copy-done
  177.4 2.0 %copy.43 = bf16[8,2048,128]{2,1,0:T(8,128)(2,1)} copy(bf16[8,2048,128]{2,1,0:T(8,128)(2,1)S(1)} %bitcast.35) | data formatting | bytes 8388608
  (3 shorter events, 0.0 us)
Async XLA Ops:
  171.5 5.9 %copy-start = (bf16[8,2,2,2,256,128]{5,4,3,2,1,0:T(8,128)(2,1)S(1)}, bf16[8,2,2,2,256,128]{5,4,3,2,1,0:T(8,128)(2,1)}, u32[]{:S(2)}) copy-start(bf16[8,2,2,2,256,128]{5,4,3,2,1,0:T(8,128)(2,1)} %get-tuple-element.14) | copy-start | bytes 12582916

commit v4 on v2

--- a/solution.py
+++ b/solution.py
@@ -31,8 +31,17 @@
 
 
 def one_hot(wanted, first, shape, axis):
-    names = lax.broadcasted_iota(jnp.int32, shape, axis) + first
-    return jnp.where(names == wanted, 1.0, 0.0).astype(jnp.bfloat16)
+    small = lambda x: x.astype(jnp.float32).astype(jnp.bfloat16)
+    size = min(shape[axis], 256)
+    part = shape[:axis] + (size,) + shape[axis + 1 :]
+    names = small(lax.broadcasted_iota(jnp.int32, part, axis))
+    one, zero = jnp.ones(part, jnp.bfloat16), jnp.zeros(part, jnp.bfloat16)
+    hots = []
+    for start in range(first, first + shape[axis], size):
+        local = wanted - start
+        local = small(jnp.where((local >= 0) & (local < size), local, -1))
+        hots.append(jnp.where(names == local, one, zero))
+    return jnp.concatenate(hots, axis=axis)
 
 
 def tables_kernel(

time: 178 us -> 179 us (level)
  no operation moved by 1% of the time
where the time goes in v4:
time: 179 us; the launch traced here: 178 us
  Pallas kernels  155 us (87%)
  local copies, waits for them, and re-layouts  13.1 us (7%)
  matrix products  4.84 us (3%)
  other arithmetic  3.91 us (2%)
    pallas_call x1, Pallas kernels, tables_call(): pl.pallas_call(functools.partial(tables_kernel, n, levels), out_shape=(ja...  128 us
    pallas_call x1, Pallas kernels, rank_call(): pl.pallas_call(functools.partial(rank_kernel, n_row, n, levels), out_shap...  27.7 us
    unnamed x8, local copies, waits for them, and re-layouts  8.62 us
    dot_general x1, matrix products, per_device(): jnp.einsum('tsk,ste->tke', placed.astype(jnp.bfloat16), pooled, preferred...  4.56 us

profile of v4, /device:TPU:0, one launch (start us, length us, event | category | flops | bytes accessed | tf_op | source)
XLA Modules:
  0.0 177.9 jit_solution(8521325788513346958)
XLA Ops:
  0.6 0.7 multiply_add_fusion
  1.4 0.7 copy.38
  2.1 0.3 fusion.4
  2.4 0.7 reshape_add_fusion
  3.2 1.6 select_reduce_fusion
  4.8 0.1 reshape.139
  4.9 0.6 copy.36
  5.5 1.4 broadcast_in_dim.35.qacc_ref
  6.9 1.5 broadcast_in_dim.36.racc_ref
  8.4 27.7 %shard_map.147 = (bf16[512,1024]{1,0:T(8,128)(2,1)}, s32[8,8,96]{2,1,0:T(8,128)}) custom-call(bf16[512,1024]{1,0:T(8,128)(2,1)} %feats_ref.1, bf16[512,1024]{1,0:T(8,128)(2,1)} %cotan_ref.1, bf16[1024,512]{1,0:T(8,128)(2,1)} %in_ref.1, bf16[1024,512]{1,0:T(8,128)(2,1)} %out_ref.1, f32[1,1024]{1,0:T(1,128)} %bitcast.44, s32[8,8,96]{2,1,0:T(8,128)} %bitcast.37), custom_call_target="tpu_custom_call" | custom-call | tf_op jit(solution)/shard_map/pallas_call | solution.py:380
  36.0 0.8 copy.20
  36.8 0.1 reshape.142
  36.9 0.1 and_select_fusion.1
  37.1 0.7 pad_add_fusion.rows_ref
  37.7 4.6 %fusion.2 = bf16[8,768,128]{2,1,0:T(8,128)(2,1)} fusion(s32[8,512]{1,0:T(8,128)S(1)} %bitcast.39, bf16[512,1024]{1,0:T(8,128)(2,1)} %get-tuple-element.10), kind=kOutput, calls=%fused_computation.4 | convolution fusion | flops 809238528 | bytes 2637824 | tf_op jit(solution)/shard_map/tsk,ste->tke/dot_general | solution.py:437
  42.3 127.7 %shard_map.148 = (bf16[8,1024,128]{2,1,0:T(8,128)(2,1)}, f32[8,1,1024]{2,1,0:T(1,128)}, bf16[8,2,2,2,256,128]{5,4,3,2,1,0:T(8,128)(2,1)}, f32[8,1,256]{2,1,0:T(1,128)}) custom-call(bf16[8,8,96,128]{3,2,1,0:T(8,128)(2,1)} %bitcast.36, s32[8,2,768]{2,1,0:T(2,128)} %pad_add_fusion.rows_ref, bf16[8,1024,128]{2,1,0:T(8,128)(2,1)} %slab_ref.1, ...), custom_call_target="tpu_custom_call" | custom-call | tf_op jit(solution)/shard_map/pallas_call | solution.py:225
  170.0 0.0 copy-start
  170.0 1.4 copy.39
  171.4 1.4 copy.35
  172.8 3.1 %copy.42 = bf16[8,1024,128]{2,1,0:T(8,128)(2,1)} copy(bf16[8,1024,128]{2,1,0:T(8,128)(2,1)} %get-tuple-element.22) | data formatting | bytes 4194304
  175.9 0.0 copy-done
  175.9 2.0 %copy.43 = bf16[8,2048,128]{2,1,0:T(8,128)(2,1)} copy(bf16[8,2048,128]{2,1,0:T(8,128)(2,1)S(1)} %bitcast.35) | data formatting | bytes 8388608
  (3 shorter events, 0.0 us)
Async XLA Ops:
  170.0 5.9 %copy-start = (bf16[8,2,2,2,256,128]{5,4,3,2,1,0:T(8,128)(2,1)S(1)}, bf16[8,2,2,2,256,128]{5,4,3,2,1,0:T(8,128)(2,1)}, u32[]{:S(2)}) copy-start(bf16[8,2,2,2,256,128]{5,4,3,2,1,0:T(8,128)(2,1)} %get-tuple-element.14) | copy-start | bytes 12582916

commit v5 on v3

--- a/solution.py
+++ b/solution.py
@@ -31,8 +31,17 @@
 
 
 def one_hot(wanted, first, shape, axis):
-    names = lax.broadcasted_iota(jnp.int32, shape, axis) + first
-    return jnp.where(names == wanted, 1.0, 0.0).astype(jnp.bfloat16)
+    small = lambda x: x.astype(jnp.float32).astype(jnp.bfloat16)
+    size = min(shape[axis], 256)
+    part = shape[:axis] + (size,) + shape[axis + 1 :]
+    names = small(lax.broadcasted_iota(jnp.int32, part, axis))
+    one, zero = jnp.ones(part, jnp.bfloat16), jnp.zeros(part, jnp.bfloat16)
+    hots = []
+    for start in range(0, shape[axis], size):
+        local = wanted - (first + start)
+        local = small(jnp.where((local >= 0) & (local < size), local, -1))
+        hots.append(jnp.where(names == local, one, zero))
+    return jnp.concatenate(hots, axis=axis)
 
 
 def tables_kernel(
@@ -184,11 +193,12 @@
 
     def half_grad(t):
         for j in range(0, n // 2, 2):
-            near = lax.broadcasted_iota(jnp.int32, (2 * share, slots), 0)
-            names = near + jnp.where(near >= share, share, 0) + (2 * j + bits[0]) * share
+            firsts = [(2 * (j + i) + bits[0]) * share for i in range(2)]
             grad = jnp.zeros((2 * share, width), jnp.float32)
             for side in range(2):
-                hot = jnp.where(names == rem_keys[side, t], 1.0, 0.0).astype(jnp.bfloat16)
+                keys = rem_keys[side, t]
+                hots = [one_hot(keys, first, (share, slots), 0) for first in firsts]
+                hot = jnp.concatenate(hots, axis=0)
                 grad += jnp.dot(hot, products[t, side], preferred_element_type=jnp.float32)
             for i in range(2):
                 where = tuple(((j + i) >> b) & 1 for b in range(levels - 2, -1, -1))

time: 181 us -> 181 us (level)
  no operation moved by 1% of the time
where the time goes in v5:
time: 181 us; the launch traced here: 179 us
  Pallas kernels  157 us (87%)
  local copies, waits for them, and re-layouts  13.1 us (7%)
  matrix products  4.84 us (3%)
  other arithmetic  3.91 us (2%)
    pallas_call x1, Pallas kernels, tables_call(): pl.pallas_call(functools.partial(tables_kernel, n, levels), out_shape=(ja...  129 us
    pallas_call x1, Pallas kernels, rank_call(): pl.pallas_call(functools.partial(rank_kernel, n_row, n, levels), out_shap...  27.7 us
    unnamed x8, local copies, waits for them, and re-layouts  8.62 us
    dot_general x1, matrix products, per_device(): jnp.einsum('tsk,ste->tke', placed.astype(jnp.bfloat16), pooled, preferred...  4.56 us

profile of v5, /device:TPU:0, one launch (start us, length us, event | category | flops | bytes accessed | tf_op | source)
XLA Modules:
  0.0 179.4 jit_solution(925888642367708196)
XLA Ops:
  0.6 0.7 multiply_add_fusion
  1.4 0.7 copy.38
  2.1 0.3 fusion.4
  2.4 0.7 reshape_add_fusion
  3.2 1.6 select_reduce_fusion
  4.8 0.1 reshape.139
  4.9 0.6 copy.36
  5.5 1.4 broadcast_in_dim.35.qacc_ref
  6.9 1.5 broadcast_in_dim.36.racc_ref
  8.4 27.7 %shard_map.147 = (bf16[512,1024]{1,0:T(8,128)(2,1)}, s32[8,8,96]{2,1,0:T(8,128)}) custom-call(bf16[512,1024]{1,0:T(8,128)(2,1)} %feats_ref.1, bf16[512,1024]{1,0:T(8,128)(2,1)} %cotan_ref.1, bf16[1024,512]{1,0:T(8,128)(2,1)} %in_ref.1, bf16[1024,512]{1,0:T(8,128)(2,1)} %out_ref.1, f32[1,1024]{1,0:T(1,128)} %bitcast.44, s32[8,8,96]{2,1,0:T(8,128)} %bitcast.37), custom_call_target="tpu_custom_call" | custom-call | tf_op jit(solution)/shard_map/pallas_call | solution.py:439
  36.1 0.8 copy.20
  36.8 0.1 reshape.142
  36.9 0.1 and_select_fusion.1
  37.1 0.7 pad_add_fusion.rows_ref
  37.8 4.6 %fusion.2 = bf16[8,768,128]{2,1,0:T(8,128)(2,1)} fusion(s32[8,512]{1,0:T(8,128)S(1)} %bitcast.39, bf16[512,1024]{1,0:T(8,128)(2,1)} %get-tuple-element.10), kind=kOutput, calls=%fused_computation.4 | convolution fusion | flops 809238528 | bytes 2637824 | tf_op jit(solution)/shard_map/tsk,ste->tke/dot_general | solution.py:496
  42.3 129.1 %shard_map.148 = (bf16[8,1024,128]{2,1,0:T(8,128)(2,1)}, f32[8,1,1024]{2,1,0:T(1,128)}, bf16[8,2,2,2,256,128]{5,4,3,2,1,0:T(8,128)(2,1)}, f32[8,1,256]{2,1,0:T(1,128)}) custom-call(bf16[8,8,96,128]{3,2,1,0:T(8,128)(2,1)} %bitcast.36, s32[8,2,768]{2,1,0:T(2,128)} %pad_add_fusion.rows_ref, bf16[8,1024,128]{2,1,0:T(8,128)(2,1)} %slab_ref.1, ...), custom_call_target="tpu_custom_call" | custom-call | tf_op jit(solution)/shard_map/pallas_call | solution.py:279
  171.4 0.0 copy-start
  171.5 1.4 copy.39
  172.9 1.4 copy.35
  174.3 3.1 %copy.42 = bf16[8,1024,128]{2,1,0:T(8,128)(2,1)} copy(bf16[8,1024,128]{2,1,0:T(8,128)(2,1)} %get-tuple-element.22) | data formatting | bytes 4194304
  177.3 0.0 copy-done
  177.3 2.0 %copy.43 = bf16[8,2048,128]{2,1,0:T(8,128)(2,1)} copy(bf16[8,2048,128]{2,1,0:T(8,128)(2,1)S(1)} %bitcast.35) | data formatting | bytes 8388608
  (3 shorter events, 0.0 us)
Async XLA Ops:
  171.4 5.9 %copy-start = (bf16[8,2,2,2,256,128]{5,4,3,2,1,0:T(8,128)(2,1)S(1)}, bf16[8,2,2,2,256,128]{5,4,3,2,1,0:T(8,128)(2,1)}, u32[]{:S(2)}) copy-start(bf16[8,2,2,2,256,128]{5,4,3,2,1,0:T(8,128)(2,1)} %get-tuple-element.14) | copy-start | bytes 12582916
